TPU v7x, 256 devices: a whole 4x4x8 slice. The times are simulated.
256 devices in a mesh: ex: 16 (over x, z_lo), par: 16 (over y, z_hi, core).
Axes of the slice: x: 4, y: 4, z: 8 (z_hi: 2, z_lo: 4; z = z_hi * 4 + z_lo), core: 2. Of those that a mesh axis runs over, the one named last changes fastest.
Arguments:
- hidden: bfloat16 [16, 512, 8192], P('ex', None, 'par'), may hold values from -6 to 6
- out_grad: bfloat16 [16, 512, 4096], P('ex', None, 'par'), may hold values from -6 to 6
- signed_scale: bfloat16 [8192, 4096], P('par', 'ex'), as said below
- indices: int32 [8192], replicated, may hold values from 0 to 33554431, as said below
Outputs:
- sketch: float32 [16, 8192], P('ex', 'par')
Inputs may be any that keep to these rules, and one draw needn't show every extreme that they name: `indices`: strictly increasing; entry k lies in [k * 8192 * 4096 / 8192, (k + 1) * 8192 * 4096 / 8192). `signed_scale`: each entry is plus or minus a factor between 0.2 and 4.
All inputs are finite; a program needn't handle non-finite values.
Results may differ from a plain program's by a relative error of at most 0.0003.
Values may be sent and summed in bfloat16 or wider, within the bound.
A program may use at most 64 MiB of HBM per device.

v0:
```python
import math

import jax
import jax.numpy as jnp
from jax import lax
from jax.sharding import PartitionSpec as P

D = 4096
FF = 8192
L = 512


def walsh_table(size):
    row_ids = lax.broadcasted_iota(jnp.int32, (size, size), 0)
    col_ids = lax.broadcasted_iota(jnp.int32, (size, size), 1)
    common = jnp.bitwise_and(row_ids, col_ids)
    parity = jnp.zeros((size, size), jnp.int32)
    for bit_pos in range(max(size.bit_length() - 1, 0)):
        parity = parity + jnp.bitwise_and(jnp.right_shift(common, bit_pos), 1)
    return (1 - 2 * jnp.bitwise_and(parity, 1)).astype(jnp.float32)


def factor_list(length):
    factors = []
    remaining = length
    while remaining > 128:
        factors.append(128)
        remaining = remaining // 128
    factors = [remaining] + factors
    return factors


def walsh_transform(values):
    batch_rows, length = values.shape
    inner_len = length
    for factor_len in factor_list(length):
        inner_len = inner_len // factor_len
        outer_len = length // (factor_len * inner_len)
        signs_table = walsh_table(factor_len)
        if inner_len == 1:
            values = jnp.dot(
                values.reshape(-1, factor_len), signs_table, precision=lax.Precision.HIGHEST
            )
        else:
            values = jnp.einsum(
                "bomk,mn->bonk",
                values.reshape(batch_rows, outer_len, factor_len, inner_len),
                signs_table,
                precision=lax.Precision.HIGHEST,
            )
        values = values.reshape(batch_rows, length)
    return values


def local(hidden, out_grad, signed_scale, indices):
    examples = hidden.shape[0]
    scale_full = lax.all_gather(signed_scale, "ex", axis=1, tiled=True)
    product = jnp.einsum(
        "elf,elc->efc",
        hidden,
        lax.all_gather(out_grad, "par", axis=2, tiled=True),
        preferred_element_type=jnp.float32,
    )
    weighted = product * scale_full.astype(jnp.float32)
    local_size = weighted.shape[1] * weighted.shape[2]
    coeffs = walsh_transform(weighted.reshape(examples, local_size))
    par_count = lax.axis_size("par")
    device_rank = lax.axis_index("par")
    block_size = local_size // par_count
    out_scale = 1.0 / math.sqrt(FF * D * L)
    signs_table = walsh_table(par_count)
    mixed_sums = jnp.einsum(
        "pq,eqr->epr",
        signs_table,
        lax.all_to_all(
            coeffs.reshape(examples, par_count, block_size),
            "par",
            split_axis=1,
            concat_axis=1,
            tiled=True,
        ),
        precision=lax.Precision.HIGHEST,
    )
    flattened = mixed_sums.reshape(mixed_sums.shape[0], par_count * block_size)
    owners = indices // block_size % par_count
    positions = indices // local_size * block_size + indices % block_size
    picked = jnp.take(flattened, positions, axis=1)
    picked = jnp.where((owners == device_rank)[None, :], picked, 0.0)
    shares = lax.psum_scatter(picked, "par", scatter_dimension=1, tiled=True)
    return shares * out_scale


def solution(mesh):
    in_specs = (P("ex", None, "par"), P("ex", None, "par"), P("par", "ex"), P())
    out_specs = P("ex", "par")
    return jax.shard_map(local, mesh=mesh, in_specs=in_specs, out_specs=out_specs, check_vma=False)
```

profile of v0, /device:TPU:1, one launch (start us, length us, event | category | flops | bytes accessed | tf_op | source)
XLA Modules:
  0.0 694.0 jit_solution(4173975249018665524)
XLA Ops:
  6.5 0.0 copy-start
  6.5 0.0 all-gather.3.cloned.1.call-start
  6.5 0.7 all-gather.3.cloned.1.call-update
  7.3 0.0 all-gather.5.cloned.1.call-start
  7.3 0.7 all-gather.5.cloned.1.call-update
  8.0 84.4 %all-gather.3.cloned.1.call-done = bf16[1,512,4096]{2,1,0:T(8,128)(2,1)} async-done(((bf16[1,512,256]{2,1,0:T(8,128)(2,1)}), bf16[1,512,4096]{2,1,0:T(8,128)(2,1)}) %all-gather.3.cloned.1.call-update) | async-done | bytes 4194320 | tf_op jit(solution)/shard_map/all_gather | solution.py:61
  92.4 103.3 %all-gather.5.cloned.1.call-done = bf16[512,4096]{1,0:T(8,128)(2,1)} async-done(((bf16[512,256]{1,0:T(8,128)(2,1)}), bf16[512,4096]{1,0:T(8,128)(2,1)}) %all-gather.5.cloned.1.call-update) | async-done | bytes 4194320 | tf_op jit(solution)/shard_map/all_gather | solution.py:57
  195.7 0.0 copy-done
  195.7 9.1 %convert_multiply_fusion = f32[512,4096]{1,0:T(8,128)} fusion(bf16[512,4096]{1,0:T(8,128)(2,1)} %all-gather.5.cloned.1.call-done, bf16[1,512,4096]{2,1,0:T(8,128)(2,1)} %all-gather.3.cloned.1.call-done, bf16[1,512,512]{2,1,0:T(8,128)(2,1)S(1)} %copy-done), kind=kOutput, calls=%fused_computation.6 | convolution fusion | flops 2151677952 | bytes 17301504 | tf_op jit(solution)/shard_map/elf,elc->efc/dot_general | solution.py:58
  204.7 10.5 %reshape.42 = f32[128,16384]{1,0:T(8,128)} reshape(f32[512,4096]{1,0:T(8,128)} %convert_multiply_fusion) | data formatting | bytes 16777216 | tf_op jit(solution)/shard_map/reshape.6
  215.3 9.0 %copy.5 = f32[16384,128]{1,0:T(8,128)} copy(f32[16384,128]{0,1:T(8,128)} %bitcast.38) | data formatting | bytes 16777216 | tf_op jit(solution)/shard_map/bomk,mn->bonk/dot_general | solution.py:45
  224.3 10.4 %fusion.11 = f32[128,128,128]{2,0,1:T(8,128)S(1)} fusion(f32[128,128,128]{2,1,0:T(8,128)} %bitcast.39), kind=kOutput, calls=%fused_computation.12 | convolution fusion | flops 3221635072 | bytes 16777216 | tf_op jit(solution)/shard_map/bomk,mn->bonk/dot_general | solution.py:45
  234.7 12.5 %fusion.3 = f32[128,128,128]{2,0,1:T(8,128)S(1)} fusion(f32[128,128,128]{2,0,1:T(8,128)S(1)} %fusion.11), kind=kOutput, calls=%fused_computation.4 | convolution fusion | flops 3221635072 | bytes 16777216 | tf_op jit(solution)/shard_map/bomk,mn->bonk/dot_general | solution.py:45
  247.2 9.1 %fusion.14 = f32[16384,128]{1,0:T(8,128)} fusion(f32[16384,128]{1,0:T(8,128)S(1)} %bitcast.37), kind=kOutput, calls=%fused_computation.15 | convolution fusion | flops 3221635072 | bytes 16777216 | tf_op jit(solution)/shard_map/dot_general | solution.py:41
  256.3 0.0 copy-start.2
  256.3 12.9 %all-to-all-start = ((f32[1,16,131072]{2,0,1:T(1,128)}), f32[1,16,131072]{2,0,1:T(1,128)}, u32[]{:S(2)}, u32[]{:S(2)}) async-start(f32[1,16,131072]{2,0,1:T(1,128)} %bitcast.36), calls=%async_computation | async-start | bytes 16777216 | tf_op jit(solution)/shard_map/all_to_all | solution.py:75
  269.2 0.0 reduce-scatter.4.cloned.1.call-start
  269.2 0.0 copy-done.2
  269.3 118.9 %all-to-all-done = f32[1,16,131072]{2,0,1:T(1,128)} async-done(((f32[1,16,131072]{2,0,1:T(1,128)}), f32[1,16,131072]{2,0,1:T(1,128)}, u32[]{:S(2)}, u32[]{:S(2)}) %all-to-all-start) | async-done | bytes 8388640 | tf_op jit(solution)/shard_map/all_to_all | solution.py:75
  388.2 15.7 %fusion.6 = f32[2,1024,8,128]{3,2,1,0:T(8,128)S(1)} fusion(f32[1,16,131072]{2,0,1:T(1,128)} %all-to-all-done), kind=kOutput, calls=%fused_computation.8 | convolution fusion | flops 402657280 | bytes 16777216 | tf_op jit(solution)/shard_map/pq,eqr->epr/dot_general | solution.py:72
  404.0 4.8 copy.11
  408.8 0.0 copy-start.1
  408.8 96.3 %gather_fusion = f32[8192]{0:T(1024)S(1)} fusion(f32[2097152]{0:T(1024)} %bitcast.35, s32[8192]{0:T(1024)S(1)} %broadcast_clamp_fusion), kind=kCustom, calls=%fused_computation | custom fusion | bytes 98304 | tf_op jit(solution)/shard_map/jit(_take)/gather | solution.py:87
  505.1 0.1 select_select_fusion
  505.2 2.6 copy.8
  507.8 0.0 reduce-scatter.4.cloned.1.call-update
  507.8 178.0 %reduce-scatter.4.cloned.1.call-done = f32[512,1]{1,0:T(8,128)} async-done(((f32[8192,1]{1,0:T(8,128)}), f32[512,1]{1,0:T(8,128)}) %reduce-scatter.4.cloned.1.call-update) | async-done | bytes 2064
  685.8 1.1 copy.9
  686.9 0.6 broadcast_multiply_fusion
  687.5 0.0 copy-done.1
  (1 shorter events, 0.0 us)
Async XLA Ops:
  6.5 189.1 %copy-start = (bf16[1,512,512]{2,1,0:T(8,128)(2,1)S(1)}, bf16[1,512,512]{2,1,0:T(8,128)(2,1)}, u32[]{:S(2)}) copy-start(bf16[1,512,512]{2,1,0:T(8,128)(2,1)} %param.4) | copy-start | bytes 1572868
  6.5 85.9 %all-gather.3.cloned.1.call-start = ((), (), s32[]{:S(2)}) async-start(), calls=%async_computation.2 | async-start | bytes 4456448 | tf_op jit(solution)/shard_map/all_gather | solution.py:61
  7.3 188.4 %all-gather.5.cloned.1.call-start = ((), (), s32[]{:S(2)}) async-start(), calls=%async_computation.3 | async-start | bytes 4456448 | tf_op jit(solution)/shard_map/all_gather | solution.py:57
  256.3 13.0 %copy-start.2 = (s32[8192]{0:T(1024)S(1)}, s32[8192]{0:T(1024)}, u32[]{:S(2)}) copy-start(s32[8192]{0:T(1024)} %param.7) | copy-start | bytes 98308
  256.3 131.9 %all-to-all-start = ((f32[1,16,131072]{2,0,1:T(1,128)}), f32[1,16,131072]{2,0,1:T(1,128)}, u32[]{:S(2)}, u32[]{:S(2)}) async-start(f32[1,16,131072]{2,0,1:T(1,128)} %bitcast.36), calls=%async_computation | async-start | bytes 16777216 | tf_op jit(solution)/shard_map/all_to_all | solution.py:75
  269.2 416.6 %reduce-scatter.4.cloned.1.call-start = ((), (), s32[]{:S(2)}) async-start(), calls=%async_computation.4 | async-start | bytes 4456448
  408.8 278.7 %copy-start.1 = (bf16[1,512,512]{2,1,0:T(8,128)(2,1)S(1)}, bf16[1,512,512]{2,1,0:T(8,128)(2,1)}, u32[]{:S(2)}) copy-start(bf16[1,512,512]{2,1,0:T(8,128)(2,1)} %param.4) | copy-start | bytes 1572868
Sparse Core Ops, SparseCore 0:
  9.9 82.4 all-gather.2
  94.1 101.5 all-gather.4
  507.9 177.8 reduce-scatter.3
where the time goes:
time: 698 us; the launch traced here: 694 us
  waiting for transfers between devices  486 us (70%)
  local copies, waits for them, and re-layouts  124 us (18%)
  matrix products  56.8 us (8%)
  between operations  13.2 us (2%)
  starting transfers between devices  13 us (2%)
    unnamed x4, waiting for transfers between devices  179 us
    all_to_all x1, waiting for transfers between devices, local(): lax.all_to_all(coeffs.reshape(examples, par_count, block_size), 'par', sp...  119 us
    all_gather x1, waiting for transfers between devices, local(): scale_full = lax.all_gather(signed_scale, 'ex', axis=1, tiled=True)  103 us
    gather x1, local copies, waits for them, and re-layouts, local(): picked = jnp.take(flattened, positions, axis=1)  96.3 us
    all_gather x1, waiting for transfers between devices, local(): lax.all_gather(out_grad, 'par', axis=2, tiled=True)  84.4 us
    dot_general x2, matrix products, walsh_transform(): jnp.einsum('bomk,mn->bonk', values.reshape(batch_rows, outer_len, factor_...  22.9 us
    dot_general x1, matrix products, local(): jnp.einsum('pq,eqr->epr', signs_table, lax.all_to_all(coeffs.reshape(exam...  15.7 us
  transfers between devices with their start and end apart: 4, of which 4 were waited for; matrix products, arithmetic and copies ran while one was open for 0% of the time, Pallas kernels for 0%

commit v1 on v0

v1 whole, which is shorter than its diff:
```python
import jax
import jax.numpy as jnp
from jax import lax
from jax.experimental import pallas as pl
from jax.experimental.pallas import tpu as pltpu
from jax.sharding import PartitionSpec as P

MESH = pl.DeviceIdType.MESH
TOKENS = 512
ROWS = 512
COLS = 256
SCALE = 2.0**-17


def parity(bits):
    bits = bits ^ (bits >> 4)
    bits = bits ^ (bits >> 2)
    bits = bits ^ (bits >> 1)
    return bits & 1


def device(x, y, zh, zl, c):
    return (x * 4 + zl, (y * 2 + zh) * 2 + c)


def kernel(hid_hbm, og_hbm, sc_hbm, idx_hbm, out_ref, hid, hid_t, s_buf, o_buf, walsh, idx_rows, idx_wide, idx_cols, acc, red_out, red_in,
           hid_sem, s_sem, o_sem, idx_sem, red_sem, hid_send, s_send, o_send, sx_send, oy_send, oc_send, red_send):
    ex = lax.axis_index("ex")
    par = lax.axis_index("par")
    x, zl = ex // 4, ex % 4
    y, zh, c = par // 4, (par // 2) % 2, par % 2
    zl_lo, zl_hi = zl % 2, zl // 2
    other_zl = zl_hi * 2 + 1 - zl_lo
    s_self = zl_hi == zl_lo
    o_self = zh == zl_lo

    def wait(ref, sem):
        pltpu.make_async_copy(ref, ref, sem).wait()

    own_hid = pltpu.make_async_copy(hid_hbm.at[0], hid.at[zl_lo], hid_sem.at[zl_lo])
    own_hid.start()
    own_idx = pltpu.make_async_copy(idx_hbm, idx_rows, idx_sem)
    own_idx.start()

    barrier = pltpu.get_barrier_semaphore()

    def greet(*place):
        pl.semaphore_signal(barrier, inc=1, device_id=device(*place), device_id_type=MESH)

    greet(x, y, zh, other_zl, c)
    for step in (1, 2, 3):
        greet((x + step) % 4, y, zh, zl, c)
        greet(x, (y + step) % 4, zh, zl, c)
    greet(x, y, zh, zl, 1 - c)
    for d3 in (0, 1):
        source = zl_lo * 2 + d3

        @pl.when(source != zl)
        def _():
            greet(x, y, zh, source, c)

    for e in (0, 1):
        source_zl = zl_hi * 2 + e

        @pl.when(jnp.logical_or(source_zl != zl, zh != zl_lo))
        def _():
            greet(x, y, zl_lo, source_zl, c)

    def greet_group(step, carry):
        there = (par + step) % 16
        pl.semaphore_signal(barrier, inc=1, device_id=(ex, there), device_id_type=MESH)
        return carry

    def greet_other(step, carry):
        there = (par + step) % 16
        pl.semaphore_signal(barrier, inc=1, device_id=(x * 4 + other_zl, there), device_id_type=MESH)
        return carry

    lax.fori_loop(1, 16, greet_group, 0)
    lax.fori_loop(0, 16, greet_other, 0)
    count = 8 + 2 + 2 + 31 - jnp.where(s_self, 1, 0) - jnp.where(o_self, 1, 0)
    pl.semaphore_wait(barrier, count)

    def to_z(src, dst, zh_to, zl_to, send, recv):
        stays = jnp.logical_and(zh_to == zh, zl_to == zl)

        @pl.when(stays)
        def _():
            pltpu.make_async_copy(src, dst, recv).start()

        @pl.when(jnp.logical_not(stays))
        def _():
            pltpu.make_async_remote_copy(src, dst, send, recv, device_id=device(x, y, zh_to, zl_to, c), device_id_type=MESH).start()

    for t in (0, 1):
        to_z(og_hbm.at[0], o_buf.at[zl_lo, y, c], t, zl_hi * 2 + zh, o_send.at[t], o_sem.at[zl_lo, y, c])
        to_z(sc_hbm, s_buf.at[x, zl_lo], zh, t * 2 + zl_hi, s_send.at[t], s_sem.at[x, zl_lo])
    hid_copy = pltpu.make_async_remote_copy(
        hid_hbm.at[0], hid.at[zl_lo], hid_send, hid_sem.at[zl_lo], device_id=device(x, y, zh, other_zl, c), device_id_type=MESH
    )
    hid_copy.start()

    rows = lax.broadcasted_iota(jnp.int32, (COLS, COLS), 0)
    cols = lax.broadcasted_iota(jnp.int32, (COLS, COLS), 1)
    walsh[...] = (1 - 2 * parity(rows & cols)).astype(jnp.float32).astype(jnp.bfloat16)
    acc[...] = jnp.zeros_like(acc)
    own_idx.wait()
    idx_wide[...] = jnp.zeros_like(idx_wide)
    for j in range(16):
        idx_wide[j : j + 1, :] = idx_rows[pl.ds(j * ROWS, ROWS)].reshape(1, ROWS) & 4095
    idx_cols[...] = idx_wide[...].T
    own_hid.wait()
    hid_t[zl_lo] = hid[zl_lo].T

    def s_copy(d3, step):
        return pltpu.make_async_remote_copy(
            s_buf.at[x, d3], s_buf.at[x, d3], sx_send.at[d3, step - 1], s_sem.at[x, d3],
            device_id=device((x + step) % 4, y, zh, zl, c), device_id_type=MESH,
        )

    def o_copy(e, step):
        return pltpu.make_async_remote_copy(
            o_buf.at[e, y, c], o_buf.at[e, y, c], oy_send.at[e, step - 1], o_sem.at[e, y, c],
            device_id=device(x, (y + step) % 4, zh, zl, c), device_id_type=MESH,
        )

    def sibling_copy(e, d1):
        return pltpu.make_async_remote_copy(
            o_buf.at[e, d1, c], o_buf.at[e, d1, c], oc_send.at[e, d1], o_sem.at[e, d1, c],
            device_id=device(x, y, zh, zl, 1 - c), device_id_type=MESH,
        )

    for d3 in (0, 1):
        wait(s_buf.at[x, d3], s_sem.at[x, d3])
        for step in (2, 1, 3):
            s_copy(d3, step).start()
    for e in (0, 1):
        wait(o_buf.at[e, y, c], o_sem.at[e, y, c])
        for step in (2, 1, 3):
            o_copy(e, step).start()
        sibling_copy(e, y).start()

    def tile(e, d1, d3):
        grad = jnp.dot(hid_t[e], o_buf[e, d1, d3], preferred_element_type=jnp.float32)
        weighted = grad * s_buf[d1, d3].astype(jnp.float32)
        top, low = weighted[: ROWS // 2], weighted[ROWS // 2 :]
        for half, part in ((0, top + low), (1, top - low)):
            hi = part.astype(jnp.bfloat16)
            lo = (part - hi.astype(jnp.float32)).astype(jnp.bfloat16)
            mixed = jnp.dot(walsh[...], hi, preferred_element_type=jnp.float32)
            mixed += jnp.dot(walsh[...], lo, preferred_element_type=jnp.float32)
            hi = mixed.astype(jnp.bfloat16)
            lo = (mixed - hi.astype(jnp.float32)).astype(jnp.bfloat16)
            mixed = jnp.dot(hi, walsh[...], preferred_element_type=jnp.float32)
            mixed += jnp.dot(lo, walsh[...], preferred_element_type=jnp.float32)
            span = pl.ds(half * COLS, COLS)
            column = idx_cols[span, :]
            lane = column & 127
            left = jnp.take_along_axis(mixed[:, :128], lane, axis=1)
            right = jnp.take_along_axis(mixed[:, 128:], lane, axis=1)
            block = d1 * 4 + zl_lo * 2 + d3
            odd = parity((column >> 8) & block)
            value = jnp.where((column & 128) == 0, left, right)
            acc[e, span, :] += jnp.where(odd == 0, value, -value)

    def columns(step, carry):
        d1 = (y + step) % 4
        for e in (0, 1):

            @pl.when(step > 0)
            def _():
                wait(o_buf.at[e, d1, c], o_sem.at[e, d1, c])
                sibling_copy(e, d1).start()

        for d3 in (0, 1):

            @pl.when(d1 != x)
            def _():
                wait(s_buf.at[d1, d3], s_sem.at[d1, d3])

        for e in (0, 1):
            wait(o_buf.at[e, d1, 1 - c], o_sem.at[e, d1, 1 - c])

        @pl.when(step == 0)
        def _():
            wait(hid.at[1 - zl_lo], hid_sem.at[1 - zl_lo])
            hid_t[1 - zl_lo] = hid[1 - zl_lo].T

        def pair(at, carry):
            tile(at // 2, d1, at % 2)
            return carry

        lax.fori_loop(0, 4, pair, 0)
        return carry

    lax.fori_loop(0, 4, columns, 0)

    for e in (0, 1):
        lines = acc[e].T
        j = lax.broadcasted_iota(jnp.int32, (16, 128), 0)
        sign = jnp.where(parity(j & par) == 0, SCALE, -SCALE)
        for q in range(4):
            red_out[e, :, q, :] = lines[:16, q * 128 : (q + 1) * 128] * sign

    own_slot = zl_lo * 16 + par
    other_slot = (1 - zl_lo) * 16

    def red_copy(e, ex_to, there, send):
        return pltpu.make_async_remote_copy(
            red_out.at[e, there], red_in.at[own_slot], red_send.at[send], red_sem.at[own_slot],
            device_id=(ex_to, there), device_id_type=MESH,
        )

    def send_group(step, carry):
        there = (par + step) % 16
        red_copy(zl_lo, ex, there, step).start()
        return carry

    def send_other(step, carry):
        there = (par + step) % 16
        red_copy(1 - zl_lo, x * 4 + other_zl, there, 16 + step).start()
        return carry

    lax.fori_loop(0, 16, send_other, 0)
    lax.fori_loop(1, 16, send_group, 0)
    red_in[own_slot] = red_out[zl_lo, par]

    for t in (0, 1):
        zh_to, zl_to = t, zl_hi * 2 + zh

        @pl.when(jnp.logical_or(zh_to != zh, zl_to != zl))
        def _():
            wait(o_buf.at[zl_lo, y, c], o_send.at[t])

        @pl.when(t * 2 + zl_hi != zl)
        def _():
            wait(s_buf.at[x, zl_lo], s_send.at[t])

    hid_copy.wait_send()
    for step in (1, 2, 3):
        for d3 in (0, 1):
            s_copy(d3, step).wait_send()
        for e in (0, 1):
            o_copy(e, step).wait_send()

    def sibling_done(d1, carry):
        for e in (0, 1):
            sibling_copy(e, d1).wait_send()
        return carry

    lax.fori_loop(0, 4, sibling_done, 0)

    def arrived(step, carry):
        there = (par + step) % 16
        wait(red_in.at[other_slot + there], red_sem.at[other_slot + there])

        @pl.when(step > 0)
        def _():
            slot = zl_lo * 16 + there
            wait(red_in.at[slot], red_sem.at[slot])
            red_copy(zl_lo, ex, there, step).wait_send()

        red_copy(1 - zl_lo, x * 4 + other_zl, there, 16 + step).wait_send()
        return carry

    lax.fori_loop(0, 16, arrived, 0)
    total = jnp.sum(red_in[...], axis=0)
    for q in range(4):
        out_ref[:, q * 128 : (q + 1) * 128] = total[q : q + 1, :]


def local(hidden, out_grad, signed_scale, indices):
    dma = pltpu.SemaphoreType.DMA
    bf16, f32, i32 = jnp.bfloat16, jnp.float32, jnp.int32
    return pl.pallas_call(
        kernel,
        out_shape=jax.ShapeDtypeStruct((1, ROWS), f32),
        in_specs=[pl.BlockSpec(memory_space=pl.ANY)] * 4,
        out_specs=pl.BlockSpec(memory_space=pltpu.VMEM),
        scratch_shapes=[
            pltpu.VMEM((2, TOKENS, ROWS), bf16),
            pltpu.VMEM((2, ROWS, TOKENS), bf16),
            pltpu.VMEM((4, 2, ROWS, COLS), bf16),
            pltpu.VMEM((2, 4, 2, TOKENS, COLS), bf16),
            pltpu.VMEM((COLS, COLS), bf16),
            pltpu.VMEM((8192,), i32),
            pltpu.VMEM((128, ROWS), i32),
            pltpu.VMEM((ROWS, 128), i32),
            pltpu.VMEM((2, ROWS, 128), f32),
            pltpu.VMEM((2, 16, 4, 128), f32),
            pltpu.VMEM((32, 4, 128), f32),
            dma((2,)),
            dma((4, 2)),
            dma((2, 4, 2)),
            dma(()),
            dma((32,)),
            dma(()),
            dma((2,)),
            dma((2,)),
            dma((2, 3)),
            dma((2, 3)),
            dma((2, 4)),
            dma((32,)),
        ],
        compiler_params=pltpu.CompilerParams(collective_id=0, has_side_effects=True, vmem_limit_bytes=48 << 20),
        cost_estimate=pl.CostEstimate(flops=6 << 30, bytes_accessed=8 << 20, transcendentals=0),
    )(hidden, out_grad, signed_scale, indices)


def solution(mesh):
    in_specs = (P("ex", None, "par"), P("ex", None, "par"), P("par", "ex"), P())
    out_specs = P("ex", "par")
    return jax.shard_map(local, mesh=mesh, in_specs=in_specs, out_specs=out_specs, check_vma=False)
```

time: 698 us -> 94.8 us (0.14)
  waiting for transfers between devices: 486 us -> 0 us
  local copies, waits for them, and re-layouts: 124 us -> 4.28 us
  Pallas kernels: 0 us -> 90.3 us
  matrix products: 56.8 us -> 0 us
  between operations: 13.2 us -> 0.01 us
  starting transfers between devices: 13 us -> 0 us
    all_gather x2 -> x0, waiting for transfers between devices: 188 us -> none  [the longest x1 103 us: local(): scale_full = lax.all_gather(signed_scale, 'ex', axis=1, tiled=True)]
    unnamed x4 -> x0, waiting for transfers between devices: 179 us -> none
    all_to_all x1 -> x0, waiting for transfers between devices: 119 us -> none  [local(): lax.all_to_all(coeffs.reshape(examples, par_count, block_size), 'par', sp...]
    gather x1 -> x0, local copies, waits for them, and re-layouts: 96.3 us -> none  [local(): picked = jnp.take(flattened, positions, axis=1)]
    pallas_call x0 -> x1, Pallas kernels: none -> 90.3 us  [local(): pl.pallas_call(kernel, out_shape=jax.ShapeDtypeStruct((1, ROWS), f32), in...]
    dot_general x5 -> x0, matrix products: 56.8 us -> none  [the longest x2 22.9 us: walsh_transform(): jnp.einsum('bomk,mn->bonk', values.reshape(batch_rows, outer_len, factor_...]
    all_to_all x1 -> x0, starting transfers between devices: 12.9 us -> none  [local(): lax.all_to_all(coeffs.reshape(examples, par_count, block_size), 'par', sp...]
    another operation x1 -> x0, local copies, waits for them, and re-layouts: 10.5 us -> none
  transfers between devices with their start and end apart: 4 -> 0, of which waited for: 4 -> 0; matrix products, arithmetic and copies ran while one was open for 0% -> 0% of each run, Pallas kernels for 0% -> 0%
where the time goes in v1:
time: 94.8 us; the launch traced here: 94.5 us
  Pallas kernels  90.3 us (95%)
  local copies, waits for them, and re-layouts  4.28 us (5%)
    pallas_call x1, Pallas kernels, local(): pl.pallas_call(kernel, out_shape=jax.ShapeDtypeStruct((1, ROWS), f32), in...  90.3 us
    unnamed x9, local copies, waits for them, and re-layouts  4.28 us

profile of v1, /device:TPU:1, one launch (start us, length us, event | category | flops | bytes accessed | tf_op | source)
XLA Modules:
  0.0 94.5 jit_solution(18018109081826026422)
XLA Ops:
  0.0 0.0 copy-start
  0.0 1.0 %copy-done = bf16[1,512,512]{2,1,0:T(8,128)(2,1)S(1)} copy-done((bf16[1,512,512]{2,1,0:T(8,128)(2,1)S(1)}, bf16[1,512,512]{2,1,0:T(8,128)(2,1)}, u32[]{:S(2)}) %copy-start) | copy-done | bytes 524312
  1.0 0.0 copy-start.1
  1.0 0.9 %copy-done.1 = bf16[1,512,256]{2,1,0:T(8,128)(2,1)S(1)} copy-done((bf16[1,512,256]{2,1,0:T(8,128)(2,1)S(1)}, bf16[1,512,256]{2,1,0:T(8,128)(2,1)}, u32[]{:S(2)}) %copy-start.1) | copy-done | bytes 262168
  2.0 0.0 copy-start.2
  2.0 0.9 %copy-done.2 = bf16[512,256]{1,0:T(8,128)(2,1)S(1)} copy-done((bf16[512,256]{1,0:T(8,128)(2,1)S(1)}, bf16[512,256]{1,0:T(8,128)(2,1)}, u32[]{:S(2)}) %copy-start.2) | copy-done | bytes 262168
  2.9 0.0 copy-start.3
  2.9 0.8 copy-done.3
  3.7 90.3 %shard_map.46 = f32[1,512]{1,0:T(1,128)S(1)} custom-call(bf16[1,512,512]{2,1,0:T(8,128)(2,1)S(1)} %copy-done, bf16[1,512,256]{2,1,0:T(8,128)(2,1)S(1)} %copy-done.1, bf16[512,256]{1,0:T(8,128)(2,1)S(1)} %copy-done.2, s32[8192]{0:T(1024)S(1)} %copy-done.3), custom_call_target="tpu_custom_call" | custom-call | flops 6442450944 | bytes 8388608 | tf_op jit(solution)/shard_map/pallas_call | solution.py:275
  94.0 0.6 copy.6
Async XLA Ops:
  0.0 1.0 %copy-start = (bf16[1,512,512]{2,1,0:T(8,128)(2,1)S(1)}, bf16[1,512,512]{2,1,0:T(8,128)(2,1)}, u32[]{:S(2)}) copy-start(bf16[1,512,512]{2,1,0:T(8,128)(2,1)} %hid_hbm.1) | copy-start | bytes 1572868
  1.0 0.9 %copy-start.1 = (bf16[1,512,256]{2,1,0:T(8,128)(2,1)S(1)}, bf16[1,512,256]{2,1,0:T(8,128)(2,1)}, u32[]{:S(2)}) copy-start(bf16[1,512,256]{2,1,0:T(8,128)(2,1)} %og_hbm.1) | copy-start | bytes 786436
  2.0 0.9 %copy-start.2 = (bf16[512,256]{1,0:T(8,128)(2,1)S(1)}, bf16[512,256]{1,0:T(8,128)(2,1)}, u32[]{:S(2)}) copy-start(bf16[512,256]{1,0:T(8,128)(2,1)} %sc_hbm.1) | copy-start | bytes 786436
  2.9 0.8 copy-start.3

commit v2 on v1

v2 whole, which is shorter than its diff:
```python
import jax
import jax.numpy as jnp
from jax import lax
from jax.experimental import pallas as pl
from jax.experimental.pallas import tpu as pltpu
from jax.sharding import PartitionSpec as P

MESH = pl.DeviceIdType.MESH
TOKENS = 512
ROWS = 512
COLS = 256
SCALE = 2.0**-17
CHUNKS = 4
WINDOW = 4
HIDDEN_AT = 3
SLAB = 512 // CHUNKS


def parity(bits):
    bits = bits ^ (bits >> 4)
    bits = bits ^ (bits >> 2)
    bits = bits ^ (bits >> 1)
    return bits & 1


def wrap(value, size):
    return jnp.where(value >= size, value - size, value)


def kernel(hid_hbm, og_hbm, sc_hbm, idx_hbm, out_ref, hid, hid_t, s_buf, o_buf, walsh, walsh_tall, idx_rows, idx_wide, idx_cols, acc,
           red_out, red_in, hid_sem, sz_sem, sx_sem, sf_sem, oz_sem, oy_sem, of_sem, sib_sem, idx_sem, red_sem, hid_send, s_send,
           o_send, sx_send, sf_send, oy_send, of_send, sib_send, red_send):
    ex = lax.axis_index("ex")
    par = lax.axis_index("par")
    x = ex // 4
    zl = ex - x * 4
    y = par // 4
    rest = par - y * 4
    zh = rest // 2
    c = rest - zh * 2
    zl_hi = zl // 2
    zl_lo = zl - zl_hi * 2
    other_lo = 1 - zl_lo
    other_ex = ex + 1 - 2 * zl_lo
    xs = [x, wrap(x + 1, 4), wrap(x + 2, 4), wrap(x + 3, 4)]
    ys = [y, wrap(y + 1, 4), wrap(y + 2, 4), wrap(y + 3, 4)]
    x_dev = [(ex + (v - x) * 4, par) for v in xs]
    y_dev = [(ex, par + (v - y) * 4) for v in ys]
    sib_dev = (ex, par + 1 - 2 * c)
    hid_dev = (other_ex, par)
    s_to = [2 * t + zl_hi for t in (0, 1)]
    s_from = [2 * zl_lo + d3 for d3 in (0, 1)]
    o_to_zl = zl_hi * 2 + zh
    o_from_zl = [zl_hi * 2 + e for e in (0, 1)]
    o_self = zh == zl_lo
    s_self = zl_hi == zl_lo

    def wait(ref, sem):
        pltpu.make_async_copy(ref, ref, sem).wait()

    def remote(src, dst, send, recv, place):
        return pltpu.make_async_remote_copy(src, dst, send, recv, device_id=place, device_id_type=MESH)

    barrier = pltpu.get_barrier_semaphore()

    def greet(place):
        pl.semaphore_signal(barrier, inc=1, device_id=place, device_id_type=MESH)

    for place in x_dev[1:] + y_dev[1:] + [sib_dev, hid_dev]:
        greet(place)
    for d3 in (0, 1):

        @pl.when(s_from[d3] != zl)
        def _():
            greet((x * 4 + s_from[d3], par))

    for e in (0, 1):

        @pl.when(jnp.logical_not(jnp.logical_and(o_self, zl_lo == e)))
        def _():
            greet((x * 4 + o_from_zl[e], y * 4 + zl_lo * 2 + c))

    for step in range(16):
        there = wrap(par + step, 16)
        if step > 0:
            greet((ex, there))
        greet((other_ex, there))

    own_hid = pltpu.make_async_copy(hid_hbm.at[0], hid.at[zl_lo], hid_sem.at[zl_lo])
    own_hid.start()
    own_idx = pltpu.make_async_copy(idx_hbm, idx_rows, idx_sem)
    own_idx.start()
    rows = lax.broadcasted_iota(jnp.int32, (COLS, COLS), 0)
    cols = lax.broadcasted_iota(jnp.int32, (COLS, COLS), 1)
    signs = (1 - 2 * parity(rows & cols)).astype(jnp.float32).astype(jnp.bfloat16)
    for half in (0, 1):
        walsh[:, half * COLS : (half + 1) * COLS] = signs
        walsh_tall[half * COLS : (half + 1) * COLS, :] = signs
    acc[...] = jnp.zeros_like(acc)
    own_idx.wait()
    idx_wide[...] = jnp.zeros_like(idx_wide)
    for j in range(16):
        idx_wide[j : j + 1, :] = idx_rows[pl.ds(j * ROWS, ROWS)].reshape(1, ROWS) & 4095
    idx_cols[...] = idx_wide[...].T
    own_hid.wait()
    hid_t[zl_lo] = hid[zl_lo].T
    pl.semaphore_wait(barrier, 43 - jnp.where(s_self, 1, 0) - jnp.where(o_self, 1, 0))

    def slab(i):
        return pl.ds(i * SLAB, SLAB)

    def along_z(i, start):
        for t in (0, 1):
            args = (og_hbm.at[0, slab(i)], o_buf.at[zl_lo, y, c, slab(i)])
            send, recv = o_send.at[t, i], oz_sem.at[zl_lo, i]
            stays = jnp.logical_and(o_self, zh == t)

            @pl.when(jnp.logical_not(stays))
            def _():
                copy = remote(*args, send, recv, (x * 4 + o_to_zl, y * 4 + t * 2 + c))
                if start:
                    copy.start()
                else:
                    copy.wait_send()

            if start:

                @pl.when(stays)
                def _():
                    pltpu.make_async_copy(*args, recv).start()

        for t in (0, 1):
            s_args = (sc_hbm.at[slab(i)], s_buf.at[x, zl_lo, slab(i)])
            s_s, s_r = s_send.at[t, i], sz_sem.at[zl_lo, i]

            @pl.when(s_to[t] != zl)
            def _():
                copy = remote(*s_args, s_s, s_r, (x * 4 + s_to[t], par))
                if start:
                    copy.start()
                else:
                    copy.wait_send()

            if start:

                @pl.when(s_to[t] == zl)
                def _():
                    pltpu.make_async_copy(*s_args, s_r).start()

    hid_copy = remote(hid_hbm.at[0], hid.at[zl_lo], hid_send, hid_sem.at[zl_lo], hid_dev)

    def sx_copy(step, i):
        ref = s_buf.at[x, :, slab(i)]
        return remote(ref, ref, sx_send, sx_sem.at[step // 2, i], x_dev[step])

    def sf_copy(step, i):
        ref = s_buf.at[xs[4 - step], step // 2, slab(i)]
        return remote(ref, ref, sf_send, sf_sem.at[step // 2, i], x_dev[step])

    def oy_copy(step, i):
        ref = o_buf.at[:, y, c, slab(i)]
        return remote(ref, ref, oy_send, oy_sem.at[step // 2, i], y_dev[step])

    def of_copy(step, i):
        ref = o_buf.at[step // 2, ys[4 - step], c, slab(i)]
        return remote(ref, ref, of_send, of_sem.at[step // 2, i], y_dev[step])

    def sib_copy(step, i):
        ref = o_buf.at[:, ys[step], c, slab(i)]
        return remote(ref, ref, sib_send, sib_sem.at[step, i], sib_dev)

    def first(i):
        for d3 in (0, 1):
            wait(s_buf.at[x, d3, slab(i)], sz_sem.at[d3, i])
        for step in (1, 3):
            sx_copy(step, i).start()
        for e in (0, 1):
            wait(o_buf.at[e, y, c, slab(i)], oz_sem.at[e, i])
        for step in (1, 3):
            oy_copy(step, i).start()
        sib_copy(0, i).start()

    def second(i):
        for step in (1, 3):
            wait(s_buf.at[xs[4 - step], :, slab(i)], sx_sem.at[step // 2, i])
            sf_copy(step, i).start()
            wait(o_buf.at[:, ys[4 - step], c, slab(i)], oy_sem.at[step // 2, i])
            of_copy(step, i).start()
            sib_copy(4 - step, i).start()

    def third(i):
        for e in (0, 1):
            wait(o_buf.at[e, ys[2], c, slab(i)], of_sem.at[e, i])
        sib_copy(2, i).start()

    for i in range(min(WINDOW, CHUNKS)):
        along_z(i, True)
    for i in range(CHUNKS + 2):
        if i < CHUNKS:
            first(i)
        if i == HIDDEN_AT:
            hid_copy.start()
        if i < CHUNKS - WINDOW:
            along_z(i, False)
            along_z(i + WINDOW, True)
        if 0 < i <= CHUNKS:
            second(i - 1)
        if i > 1:
            third(i - 2)
    for i in range(CHUNKS):
        for d3 in (0, 1):
            wait(s_buf.at[xs[2], d3, slab(i)], sf_sem.at[d3, i])

    def tile(e, d1, d3):
        grad = jnp.dot(hid_t[e], o_buf[e, d1, d3], preferred_element_type=jnp.float32)
        weighted = grad * s_buf[d1, d3].astype(jnp.float32)
        top, low = weighted[: ROWS // 2], weighted[ROWS // 2 :]
        for half, part in ((0, top + low), (1, top - low)):
            hi = part.astype(jnp.bfloat16)
            lo = (part - hi.astype(jnp.float32)).astype(jnp.bfloat16)
            mixed = jnp.dot(walsh[...], jnp.concatenate([hi, lo], axis=0), preferred_element_type=jnp.float32)
            hi = mixed.astype(jnp.bfloat16)
            lo = (mixed - hi.astype(jnp.float32)).astype(jnp.bfloat16)
            mixed = jnp.dot(jnp.concatenate([hi, lo], axis=1), walsh_tall[...], preferred_element_type=jnp.float32)
            span = pl.ds(half * COLS, COLS)
            column = idx_cols[span, :]
            lane = column & 127
            left = jnp.take_along_axis(mixed[:, :128], lane, axis=1)
            right = jnp.take_along_axis(mixed[:, 128:], lane, axis=1)
            block = d1 * 4 + zl_lo * 2 + d3
            odd = parity((column >> 8) & block)
            value = jnp.where((column & 128) == 0, left, right)
            acc[e, span, :] += jnp.where(odd == 0, value, -value)

    def column_pair(e, step):
        d1 = wrap(y + step, 4)
        for d3 in (0, 1):
            tile(e, d1, d3)

    def own_columns(step, carry):
        for i in range(CHUNKS):
            wait(o_buf.at[:, wrap(y + step, 4), 1 - c, slab(i)], sib_sem.at[step, i])
        column_pair(zl_lo, step)
        return carry

    lax.fori_loop(0, 4, own_columns, 0)

    own_slot = zl_lo * 16 + par
    other_slot = other_lo * 16

    def gather_picks(e):
        lines = acc[e].T
        j = lax.broadcasted_iota(jnp.int32, (16, 128), 0)
        sign = jnp.where(parity(j & par) == 0, SCALE, -SCALE)
        for q in range(4):
            red_out[e, :, q, :] = lines[:16, q * 128 : (q + 1) * 128] * sign

    def red_copy(e, step):
        there = wrap(par + step, 16)
        place = (jnp.where(e == zl_lo, ex, other_ex), there)
        return remote(red_out.at[e, there], red_in.at[own_slot], red_send, red_sem.at[own_slot], place)

    gather_picks(zl_lo)
    for step in range(1, 16):
        red_copy(zl_lo, step).start()
    red_in[own_slot] = red_out[zl_lo, par]

    wait(hid.at[other_lo], hid_sem.at[other_lo])
    hid_t[other_lo] = hid[other_lo].T

    def other_columns(step, carry):
        column_pair(other_lo, step)
        return carry

    lax.fori_loop(0, 4, other_columns, 0)
    gather_picks(other_lo)
    for step in range(16):
        red_copy(other_lo, step).start()

    for i in range(max(CHUNKS - WINDOW, 0), CHUNKS):
        along_z(i, False)
    hid_copy.wait_send()
    wait(s_buf.at[0:2], sx_send)
    wait(s_buf.at[0], sf_send)
    wait(s_buf.at[0:2], oy_send)
    wait(s_buf.at[0], of_send)
    wait(s_buf, sib_send)

    for step in range(16):
        there = wrap(par + step, 16)
        wait(red_in.at[other_slot + there], red_sem.at[other_slot + there])
        if step > 0:
            slot = zl_lo * 16 + there
            wait(red_in.at[slot], red_sem.at[slot])
    wait(red_in.at[0:31], red_send)
    total = jnp.sum(red_in[...], axis=0)
    for q in range(4):
        out_ref[:, q * 128 : (q + 1) * 128] = total[q : q + 1, :]


def local(hidden, out_grad, signed_scale, indices):
    dma = pltpu.SemaphoreType.DMA
    bf16, f32, i32 = jnp.bfloat16, jnp.float32, jnp.int32
    return pl.pallas_call(
        kernel,
        out_shape=jax.ShapeDtypeStruct((1, ROWS), f32),
        in_specs=[pl.BlockSpec(memory_space=pltpu.HBM)] * 4,
        out_specs=pl.BlockSpec(memory_space=pltpu.VMEM),
        scratch_shapes=[
            pltpu.VMEM((2, TOKENS, ROWS), bf16),
            pltpu.VMEM((2, ROWS, TOKENS), bf16),
            pltpu.VMEM((4, 2, ROWS, COLS), bf16),
            pltpu.VMEM((2, 4, 2, TOKENS, COLS), bf16),
            pltpu.VMEM((COLS, 2 * COLS), bf16),
            pltpu.VMEM((2 * COLS, COLS), bf16),
            pltpu.VMEM((8192,), i32),
            pltpu.VMEM((128, ROWS), i32),
            pltpu.VMEM((ROWS, 128), i32),
            pltpu.VMEM((2, ROWS, 128), f32),
            pltpu.VMEM((2, 16, 4, 128), f32),
            pltpu.VMEM((32, 4, 128), f32),
            dma((2,)),
            dma((2, CHUNKS)),
            dma((2, CHUNKS)),
            dma((2, CHUNKS)),
            dma((2, CHUNKS)),
            dma((2, CHUNKS)),
            dma((2, CHUNKS)),
            dma((4, CHUNKS)),
            dma(()),
            dma((32,)),
            dma(()),
            dma((2, CHUNKS)),
            dma((2, CHUNKS)),
            dma(()),
            dma(()),
            dma(()),
            dma(()),
            dma(()),
            dma(()),
        ],
        compiler_params=pltpu.CompilerParams(collective_id=0, has_side_effects=True, vmem_limit_bytes=56 << 20),
        cost_estimate=pl.CostEstimate(flops=6 << 30, bytes_accessed=8 << 20, transcendentals=0),
    )(hidden, out_grad, signed_scale, indices)


def solution(mesh):
    in_specs = (P("ex", None, "par"), P("ex", None, "par"), P("par", "ex"), P())
    out_specs = P("ex", "par")
    return jax.shard_map(local, mesh=mesh, in_specs=in_specs, out_specs=out_specs, check_vma=False)
```

time: 94.8 us -> 70.7 us (0.75)
  Pallas kernels: 90.3 us -> 69.3 us
  local copies, waits for them, and re-layouts: 4.28 us -> 1.26 us
    pallas_call x1, Pallas kernels: 90.3 us -> 69.3 us  [local(): pl.pallas_call(kernel, out_shape=jax.ShapeDtypeStruct((1, ROWS), f32), in...]
    unnamed x9 -> x1, local copies, waits for them, and re-layouts: 4.28 us -> 1.26 us
where the time goes in v2:
time: 70.7 us; the launch traced here: 70.6 us
  Pallas kernels  69.3 us (98%)
  local copies, waits for them, and re-layouts  1.26 us (2%)
    pallas_call x1, Pallas kernels, local(): pl.pallas_call(kernel, out_shape=jax.ShapeDtypeStruct((1, ROWS), f32), in...  69.3 us

profile of v2, /device:TPU:1, one launch (start us, length us, event | category | flops | bytes accessed | tf_op | source)
XLA Modules:
  0.0 70.6 jit_solution(1065347392566265197)
XLA Ops:
  0.0 69.3 %shard_map.46 = f32[1,512]{1,0:T(1,128)} custom-call(bf16[1,512,512]{2,1,0:T(8,128)(2,1)} %hid_hbm.1, bf16[1,512,256]{2,1,0:T(8,128)(2,1)} %og_hbm.1, bf16[512,256]{1,0:T(8,128)(2,1)} %sc_hbm.1, s32[8192]{0:T(1024)} %idx_hbm.1), custom_call_target="tpu_custom_call" | custom-call | flops 6442450944 | bytes 8388608 | tf_op jit(solution)/shard_map/pallas_call | solution.py:304
  69.3 1.3 %copy.6 = f32[1,512]{1,0:T(1,128)} copy(f32[1,512]{1,0:T(1,128)} %shard_map.46) | data formatting | bytes 4096

commit v3 on v2

--- a/solution.py
+++ b/solution.py
@@ -80,12 +80,6 @@
         def _():
             greet((x * 4 + o_from_zl[e], y * 4 + zl_lo * 2 + c))
 
-    for step in range(16):
-        there = wrap(par + step, 16)
-        if step > 0:
-            greet((ex, there))
-        greet((other_ex, there))
-
     own_hid = pltpu.make_async_copy(hid_hbm.at[0], hid.at[zl_lo], hid_sem.at[zl_lo])
     own_hid.start()
     own_idx = pltpu.make_async_copy(idx_hbm, idx_rows, idx_sem)
@@ -104,7 +98,7 @@
     idx_cols[...] = idx_wide[...].T
     own_hid.wait()
     hid_t[zl_lo] = hid[zl_lo].T
-    pl.semaphore_wait(barrier, 43 - jnp.where(s_self, 1, 0) - jnp.where(o_self, 1, 0))
+    pl.semaphore_wait(barrier, 12 - jnp.where(s_self, 1, 0) - jnp.where(o_self, 1, 0))
 
     def slab(i):
         return pl.ds(i * SLAB, SLAB)
@@ -168,6 +162,9 @@
     def sib_copy(step, i):
         ref = o_buf.at[:, ys[step], c, slab(i)]
         return remote(ref, ref, sib_send, sib_sem.at[step, i], sib_dev)
+
+    def sib_wait(step, i):
+        wait(o_buf.at[:, wrap(y + step, 4), 1 - c, slab(i)], sib_sem.at[step, i])
 
     def first(i):
         for d3 in (0, 1):
@@ -199,6 +196,8 @@
         if i < CHUNKS:
             first(i)
         if i == HIDDEN_AT:
+            for step in range(4):
+                sib_wait(step, 0)
             hid_copy.start()
         if i < CHUNKS - WINDOW:
             along_z(i, False)
@@ -238,8 +237,8 @@
             tile(e, d1, d3)
 
     def own_columns(step, carry):
-        for i in range(CHUNKS):
-            wait(o_buf.at[:, wrap(y + step, 4), 1 - c, slab(i)], sib_sem.at[step, i])
+        for i in range(1, CHUNKS):
+            sib_wait(step, i)
         column_pair(zl_lo, step)
         return carry
 

time: 70.7 us -> 69.6 us (0.984)
  Pallas kernels: 69.3 us -> 68.2 us
    pallas_call x1, Pallas kernels: 69.3 us -> 68.2 us  [local(): pl.pallas_call(kernel, out_shape=jax.ShapeDtypeStruct((1, ROWS), f32), in...]
where the time goes in v3:
time: 69.6 us; the launch traced here: 69.5 us
  Pallas kernels  68.2 us (98%)
  local copies, waits for them, and re-layouts  1.26 us (2%)
    pallas_call x1, Pallas kernels, local(): pl.pallas_call(kernel, out_shape=jax.ShapeDtypeStruct((1, ROWS), f32), in...  68.2 us

profile of v3, /device:TPU:1, one launch (start us, length us, event | category | flops | bytes accessed | tf_op | source)
XLA Modules:
  0.0 69.5 jit_solution(18061565048620621104)
XLA Ops:
  0.0 68.2 %shard_map.46 = f32[1,512]{1,0:T(1,128)} custom-call(bf16[1,512,512]{2,1,0:T(8,128)(2,1)} %hid_hbm.1, bf16[1,512,256]{2,1,0:T(8,128)(2,1)} %og_hbm.1, bf16[512,256]{1,0:T(8,128)(2,1)} %sc_hbm.1, s32[8192]{0:T(1024)} %idx_hbm.1), custom_call_target="tpu_custom_call" | custom-call | flops 6442450944 | bytes 8388608 | tf_op jit(solution)/shard_map/pallas_call | solution.py:303
  68.2 1.3 %copy.6 = f32[1,512]{1,0:T(1,128)} copy(f32[1,512]{1,0:T(1,128)} %shard_map.46) | data formatting | bytes 4096

commit v4 on v3

--- a/solution.py
+++ b/solution.py
@@ -242,7 +242,7 @@
         column_pair(zl_lo, step)
         return carry
 
-    lax.fori_loop(0, 4, own_columns, 0)
+    lax.fori_loop(0, 4, own_columns, 0, unroll=True)
 
     own_slot = zl_lo * 16 + par
     other_slot = other_lo * 16
@@ -271,7 +271,7 @@
         column_pair(other_lo, step)
         return carry
 
-    lax.fori_loop(0, 4, other_columns, 0)
+    lax.fori_loop(0, 4, other_columns, 0, unroll=True)
     gather_picks(other_lo)
     for step in range(16):
         red_copy(other_lo, step).start()

time: 69.6 us -> 67.7 us (0.973)
  Pallas kernels: 68.2 us -> 66.2 us
    pallas_call x1, Pallas kernels: 68.2 us -> 66.2 us  [local(): pl.pallas_call(kernel, out_shape=jax.ShapeDtypeStruct((1, ROWS), f32), in...]
where the time goes in v4:
time: 67.7 us; the launch traced here: 67.5 us
  Pallas kernels  66.2 us (98%)
  local copies, waits for them, and re-layouts  1.26 us (2%)
    pallas_call x1, Pallas kernels, local(): pl.pallas_call(kernel, out_shape=jax.ShapeDtypeStruct((1, ROWS), f32), in...  66.2 us

profile of v4, /device:TPU:1, one launch (start us, length us, event | category | flops | bytes accessed | tf_op | source)
XLA Modules:
  0.0 67.5 jit_solution(6391360865596186298)
XLA Ops:
  0.0 66.2 %shard_map.46 = f32[1,512]{1,0:T(1,128)} custom-call(bf16[1,512,512]{2,1,0:T(8,128)(2,1)} %hid_hbm.1, bf16[1,512,256]{2,1,0:T(8,128)(2,1)} %og_hbm.1, bf16[512,256]{1,0:T(8,128)(2,1)} %sc_hbm.1, s32[8192]{0:T(1024)} %idx_hbm.1), custom_call_target="tpu_custom_call" | custom-call | flops 6442450944 | bytes 8388608 | tf_op jit(solution)/shard_map/pallas_call | solution.py:303
  66.2 1.3 %copy.6 = f32[1,512]{1,0:T(1,128)} copy(f32[1,512]{1,0:T(1,128)} %shard_map.46) | data formatting | bytes 4096

commit v5 on v4

--- a/solution.py
+++ b/solution.py
@@ -12,7 +12,7 @@
 SCALE = 2.0**-17
 CHUNKS = 4
 WINDOW = 4
-HIDDEN_AT = 3
+HIDDEN_AT = 2
 SLAB = 512 // CHUNKS
 
 
@@ -195,10 +195,6 @@
     for i in range(CHUNKS + 2):
         if i < CHUNKS:
             first(i)
-        if i == HIDDEN_AT:
-            for step in range(4):
-                sib_wait(step, 0)
-            hid_copy.start()
         if i < CHUNKS - WINDOW:
             along_z(i, False)
             along_z(i + WINDOW, True)
@@ -206,6 +202,10 @@
             second(i - 1)
         if i > 1:
             third(i - 2)
+        if i == HIDDEN_AT:
+            for step in range(4):
+                sib_wait(step, 0)
+            hid_copy.start()
     for i in range(CHUNKS):
         for d3 in (0, 1):
             wait(s_buf.at[xs[2], d3, slab(i)], sf_sem.at[d3, i])

time: 67.7 us -> 66.8 us (0.987)
  Pallas kernels: 66.2 us -> 65.4 us
    pallas_call x1, Pallas kernels: 66.2 us -> 65.4 us  [local(): pl.pallas_call(kernel, out_shape=jax.ShapeDtypeStruct((1, ROWS), f32), in...]
where the time goes in v5:
time: 66.8 us; the launch traced here: 66.7 us
  Pallas kernels  65.4 us (98%)
  local copies, waits for them, and re-layouts  1.26 us (2%)
    pallas_call x1, Pallas kernels, local(): pl.pallas_call(kernel, out_shape=jax.ShapeDtypeStruct((1, ROWS), f32), in...  65.4 us

profile of v5, /device:TPU:1, one launch (start us, length us, event | category | flops | bytes accessed | tf_op | source)
XLA Modules:
  0.0 66.7 jit_solution(15310068784615966734)
XLA Ops:
  0.0 65.4 %shard_map.46 = f32[1,512]{1,0:T(1,128)} custom-call(bf16[1,512,512]{2,1,0:T(8,128)(2,1)} %hid_hbm.1, bf16[1,512,256]{2,1,0:T(8,128)(2,1)} %og_hbm.1, bf16[512,256]{1,0:T(8,128)(2,1)} %sc_hbm.1, s32[8192]{0:T(1024)} %idx_hbm.1), custom_call_target="tpu_custom_call" | custom-call | flops 6442450944 | bytes 8388608 | tf_op jit(solution)/shard_map/pallas_call | solution.py:303
  65.4 1.3 %copy.6 = f32[1,512]{1,0:T(1,128)} copy(f32[1,512]{1,0:T(1,128)} %shard_map.46) | data formatting | bytes 4096
